TPU v7x, 32 devices: a whole 2x2x4 slice. The times are simulated.
32 devices in a mesh: layer: 8 (over y, x, core), wave: 4 (over z).
Axes of the slice: x: 2, y: 2, z: 4, core: 2. Of those that a mesh axis runs over, the one named last changes fastest.
Arguments:
- eps_harmonics: float32 [8, 2, 255], P('layer'), may hold values from -4 to 4
- eigen_modes: float32 [8, 4, 2, 128, 128], P('layer', 'wave'), may hold values from -1 to 2
- mode_phase: float32 [8, 4, 128], P('layer', 'wave'), may hold values from -3.140625 to 3.140625
- mode_decay: float32 [8, 4, 128], P('layer', 'wave'), may hold values from 0.002 to 0.1
- retained_orders: int32 [4], P('wave'), may hold values from 64 to 128, as said below
- reflect_cotangent: float32 [4, 2, 128, 128], P('wave'), may hold values from -6 to 6
Outputs:
- eps_gradient: float32 [8, 2, 255], P('layer')
- mode_gradient: float32 [8, 4, 2, 128, 128], P('layer', 'wave')
Inputs may be any that keep to these rules, and one draw needn't show every extreme that they name: `retained_orders`: in every draw some wavelength retains all 128 orders and another retains 128 // 2.
All inputs are finite; a program needn't handle non-finite values.
Results may differ from a plain program's by a relative error of at most 0.0003.
Values sent between devices are 32-bit elements; how exact they have to be, the bound alone decides.
A program may use at most 64 MiB of HBM per device.

v0:
```python
import functools
import math

import jax
import jax.numpy as jnp
from jax import lax
from jax.experimental import pallas as pl
from jax.experimental.pallas import tpu as pltpu
from jax.sharding import PartitionSpec as P

TRANSMISSION = 0.9
LEVELS = 5
F32 = jnp.float32
BF16 = jnp.bfloat16


def split(x):
    hi = x.astype(BF16)
    return hi, (x - hi.astype(F32)).astype(BF16)


def embed(b):
    n = b.shape[0]
    return jnp.concatenate([b, jnp.concatenate([-b[:, n:], b[:, :n]], axis=1)], axis=0)


def weights(parts):
    return embed(parts[0]), embed(parts[1])


def real_dot(a, b):
    return jnp.dot(a, b, preferred_element_type=F32)


def products(lefts, weight):
    n = lefts[0][0].shape[0]
    high, low = weight
    first = real_dot(jnp.concatenate([part for left in lefts for part in left], axis=0), high)
    second = real_dot(jnp.concatenate([left[0] for left in lefts], axis=0), low)
    return [
        first[2 * i * n : (2 * i + 1) * n]
        + first[(2 * i + 1) * n : (2 * i + 2) * n]
        + second[i * n : (i + 1) * n]
        for i in range(len(lefts))
    ]


def product(left, right):
    return products([left], weights(right))[0]


def scaled(a, b):
    n = a.shape[0]
    ar, ai, br, bi = a[:, :n], a[:, n:], b[:, :n], b[:, n:]
    return jnp.concatenate([ar * br - ai * bi, ar * bi + ai * br], axis=1)


def conj_transpose(a):
    n = a.shape[0]
    return jnp.concatenate([a[:, :n].T, -a[:, n:].T], axis=1)


def spread_rows(prop):
    n = prop.shape[-1] // 2
    return jnp.broadcast_to(prop, (n, 2 * n))


def spread_columns(prop):
    n = prop.shape[-1] // 2
    rows = spread_rows(prop)
    return jnp.concatenate([rows[:, :n].T, rows[:, n:].T], axis=1)


def outer(prop):
    return scaled(spread_columns(prop), spread_rows(prop))


def series(start, base):
    starts, powers = [], []
    value, power = start, base
    for level in range(LEVELS):
        value_parts, power_parts = split(value), split(power)
        starts.append(value_parts)
        powers.append(power_parts)
        weight = weights(power_parts)
        if level + 1 < LEVELS:
            step, power = products([value_parts, power_parts], weight)
        else:
            (step,) = products([value_parts], weight)
        value = value + step
    return value, starts, powers


def series_back(starts, powers, cotangent, need_start):
    power_bar = None
    for level in reversed(range(LEVELS)):
        parts = split(cotangent)
        total = product(parts, starts[level])
        if power_bar is not None:
            bar_parts = split(power_bar)
            total = total + product(bar_parts, powers[level])
            total = total + product(powers[level], bar_parts)
        if level > 0 or need_start:
            cotangent = cotangent + product(powers[level], parts)
        power_bar = total
    return power_bar, cotangent


def order_mask(count, n):
    half = count // 2
    row = lax.broadcasted_iota(jnp.int32, (n, n), 0) - n // 2
    column = lax.broadcasted_iota(jnp.int32, (n, n), 1) - n // 2
    keep = (row >= -half) & (row < count - half) & (column >= -half) & (column < count - half)
    return keep.astype(F32)


def toeplitz_of(harm_ref, n):
    def one(part):
        rows = jnp.broadcast_to(harm_ref[part : part + 1, :], (n, 2 * n))
        rolled = pltpu.roll(rows, n + 1, 1, stride=1, stride_axis=0)
        return rolled[:, :n].T

    return jnp.concatenate([one(0), one(1)], axis=1)


def sheet_kernel(count_ref, harm_ref, mode_ref, phase_ref, decay_ref, pack_ref):
    n = mode_ref.shape[-1]
    count = count_ref[0]
    toeplitz = toeplitz_of(harm_ref, n)
    modes = jnp.concatenate([mode_ref[0], mode_ref[1]], axis=1)
    mask = order_mask(count, n) * (1.0 / (5.0 * math.sqrt(2 * n - 1)))
    coupled = product(split(toeplitz), split(modes))
    pack_ref[:n, :] = coupled * jnp.concatenate([mask, mask], axis=1)
    order = lax.broadcasted_iota(jnp.int32, (1, n), 1) - n // 2
    window = ((order >= -(count // 2)) & (order < count - count // 2)).astype(F32)
    magnitude = window * jnp.exp(-decay_ref[...])
    phase = phase_ref[...]
    prop = jnp.concatenate([magnitude * jnp.cos(phase), magnitude * jnp.sin(phase)], axis=1)
    pack_ref[n:, :] = jnp.broadcast_to(prop, (8, 2 * n))


def chain_kernel(
    layers, count_ref, harm_ref, mode_ref, cot_ref, pack_ref, eps_ref, grad_ref,
    below, back, left, right, bar,
):
    n = mode_ref.shape[-1]
    through = TRANSMISSION
    both = through * through
    me = lax.axis_index("layer")

    def sheet(i):
        return pack_ref[i, :n, :]

    def prop(i):
        return pack_ref[i, n : n + 1, :]

    below[...] = scaled(outer(prop(layers - 2)), sheet(layers - 1))

    def go_up(step, carry):
        i = layers - 2 - step
        here = sheet(i)
        start = below[...]
        base = product(split(here), split(start))
        value, _, _ = series(start, base)
        below[...] = scaled(outer(prop(i - 1)), here + both * value)
        return carry

    lax.fori_loop(0, jnp.maximum(layers - 2 - me, 0), go_up, 0)

    @pl.when(me == layers - 1)
    def _():
        below[...] = jnp.zeros_like(below)

    unit = (
        lax.broadcasted_iota(jnp.int32, (n, n), 0) == lax.broadcasted_iota(jnp.int32, (n, n), 1)
    ).astype(F32)
    unit = jnp.concatenate([unit, unit], axis=1)
    back[...] = scaled(outer(prop(0)), sheet(0))
    left[...] = through * unit * prop(0)
    right[...] = through * unit * prop(0)

    def go_down(i, carry):
        here = split(sheet(i))
        value, into, out = back[...], left[...], right[...]
        value_parts = split(value)
        power = product(here, value_parts)
        other = product(value_parts, here)
        for level in range(LEVELS):
            power_parts, other_parts = split(power), split(other)
            weight = weights(power_parts)
            last = level + 1 == LEVELS
            lefts = [split(value), split(into)] + ([] if last else [power_parts])
            steps = products(lefts, weight)
            value, into = value + steps[0], into + steps[1]
            out = out + product(other_parts, split(out))
            if not last:
                power = steps[2]
                other = product(other_parts, other_parts)
        p = prop(i)
        back[...] = scaled(outer(p), sheet(i) + both * value)
        left[...] = through * scaled(into, spread_rows(p))
        right[...] = through * scaled(spread_columns(p), out)
        return carry

    lax.fori_loop(1, jnp.maximum(me, 1), go_down, 0)

    here = sheet(me)
    start = below[...]
    base = product(split(here), split(start))
    value, starts, powers = series(start, base)
    reflection = here + both * value
    bar[...] = conj_transpose(jnp.concatenate([cot_ref[0], cot_ref[1]], axis=1))

    @pl.when(me > 0)
    def _():
        above = split(back[...])
        above_base = product(above, split(reflection))
        _, above_starts, above_powers = series(reflection, above_base)
        inner = product(split(product(split(right[...]), split(bar[...]))), split(left[...]))
        base_bar, start_bar = series_back(above_starts, above_powers, inner, True)
        bar[...] = start_bar + product(split(base_bar), above)

    sheet_bar = bar[...]
    base_bar, _ = series_back(starts, powers, both * sheet_bar, False)
    sheet_bar = sheet_bar + product(split(start), split(base_bar))
    mask = order_mask(count_ref[0], n) * (1.0 / (5.0 * math.sqrt(2 * n - 1)))
    coupled_bar = split(sheet_bar * jnp.concatenate([mask, mask], axis=1))
    modes = jnp.concatenate([mode_ref[0], mode_ref[1]], axis=1)
    mode_bar = conj_transpose(product(coupled_bar, split(toeplitz_of(harm_ref, n))))
    grad_ref[0] = mode_bar[:, :n]
    grad_ref[1] = mode_bar[:, n:]
    flip = (
        lax.broadcasted_iota(jnp.int32, (n, n), 0) + lax.broadcasted_iota(jnp.int32, (n, n), 1)
        == n - 1
    ).astype(F32).astype(BF16)
    flipped = tuple(real_dot(flip, part).astype(BF16) for part in split(modes))
    toeplitz_bar = product(flipped, coupled_bar)
    zeros = jnp.zeros((n, n), F32)

    def fold(part):
        wide = jnp.concatenate([part, zeros], axis=1)
        rolled = pltpu.roll(wide, 0, 1, stride=1, stride_axis=0)
        return jnp.sum(rolled, axis=0, keepdims=True)

    eps_ref[0:1, :] = fold(toeplitz_bar[:, :n])
    eps_ref[1:2, :] = -fold(toeplitz_bar[:, n:])


def per_device(
    layers, eps_harmonics, eigen_modes, mode_phase, mode_decay, retained_orders, reflect_cotangent
):
    n = eigen_modes.shape[-1]
    vmem = pl.BlockSpec(memory_space=pltpu.VMEM)
    smem = pl.BlockSpec(memory_space=pltpu.SMEM)
    params = pltpu.CompilerParams(vmem_limit_bytes=48 * 1024 * 1024)
    harmonics = jnp.pad(eps_harmonics[0], ((0, 0), (0, 1)))
    modes = eigen_modes[0, 0]
    pack = pl.pallas_call(
        sheet_kernel,
        out_shape=jax.ShapeDtypeStruct((n + 8, 2 * n), F32),
        in_specs=[smem] + [vmem] * 4,
        out_specs=vmem,
        compiler_params=params,
        name="sheet",
    )(retained_orders, harmonics, modes, mode_phase[0], mode_decay[0])
    packs = lax.all_gather(pack, "layer")
    eps_part, grad = pl.pallas_call(
        functools.partial(chain_kernel, layers),
        out_shape=(
            jax.ShapeDtypeStruct((2, 2 * n), F32),
            jax.ShapeDtypeStruct((2, n, n), F32),
        ),
        in_specs=[smem] + [vmem] * 4,
        out_specs=(vmem, vmem),
        scratch_shapes=[pltpu.VMEM((n, 2 * n), F32) for _ in range(5)],
        compiler_params=params,
        name="chain",
    )(retained_orders, harmonics, modes, reflect_cotangent[0], packs)
    eps_grad = lax.psum(eps_part, "wave")[:, : 2 * n - 1]
    return eps_grad[None], grad[None, None]


def solution(mesh):
    placed = (
        P("layer", None, None),
        P("layer", "wave", None, None, None),
        P("layer", "wave", None),
        P("layer", "wave", None),
        P("wave"),
        P("wave", None, None, None),
    )
    return jax.shard_map(
        functools.partial(per_device, mesh.shape["layer"]),
        mesh=mesh,
        in_specs=placed,
        out_specs=(P("layer", None, None), P("layer", "wave", None, None, None)),
        check_vma=False,
    )
```

profile of v0, /device:TPU:7, one launch (start us, length us, event | category | flops | bytes accessed | tf_op | source)
XLA Modules:
  0.0 78.8 jit_solution(9152955967431437356)
XLA Ops:
  7.2 0.0 all-gather.3.cloned.1.call-start
  7.9 0.7 pad.4.harm_ref
  8.5 0.0 copy-start.1
  8.5 0.9 %copy-done.1 = f32[1,1,2,128,128]{4,3,2,1,0:T(8,128)S(1)} copy-done((f32[1,1,2,128,128]{4,3,2,1,0:T(8,128)S(1)}, f32[1,1,2,128,128]{4,3,2,1,0:T(8,128)}, u32[]{:S(2)}) %copy-start.1) | copy-done | bytes 131096
  9.4 0.0 copy-start.4
  9.5 0.7 copy-done.4
  10.1 0.0 copy-start.5
  10.1 0.7 copy-done.5
  10.8 1.0 %sheet.1 = f32[136,256]{1,0:T(8,128)} custom-call(s32[1]{0:T(128)S(6)} %copy.8.count_ref, f32[2,256]{1,0:T(2,128)S(1)} %pad.4.harm_ref, f32[2,128,128]{2,1,0:T(8,128)S(1)} %bitcast.10, f32[1,128]{1,0:T(1,128)S(1)} %bitcast.13, f32[1,128]{1,0:T(1,128)S(1)} %bitcast.14), custom_call_target="tpu_custom_call" | custom-call | tf_op jit(solution)/shard_map/sheet/pallas_call | solution.py:258
  11.8 0.0 all-gather.3.cloned.1.call-update
  11.8 24.6 %all-gather.3.cloned.1.call-done = f32[1088,256]{1,0:T(8,128)} async-done(((f32[136,256]{1,0:T(8,128)}), f32[1088,256]{1,0:T(8,128)}) %all-gather.3.cloned.1.call-update) | async-done | bytes 1114128 | tf_op jit(solution)/shard_map/all_gather | solution.py:266
  36.5 0.0 copy-start
  36.5 1.2 %copy-done = f32[1088,256]{1,0:T(8,128)S(1)} copy-done((f32[1088,256]{1,0:T(8,128)S(1)}, f32[1088,256]{1,0:T(8,128)}, u32[]{:S(2)}) %copy-start) | copy-done | bytes 1114136
  37.7 0.0 copy-start.2
  37.7 0.9 %copy-done.2 = f32[1,1,2,128,128]{4,3,2,1,0:T(8,128)S(1)} copy-done((f32[1,1,2,128,128]{4,3,2,1,0:T(8,128)S(1)}, f32[1,1,2,128,128]{4,3,2,1,0:T(8,128)}, u32[]{:S(2)}) %copy-start.2) | copy-done | bytes 131096
  38.6 0.0 copy-start.3
  38.6 0.9 %copy-done.3 = f32[1,2,128,128]{3,2,1,0:T(8,128)S(1)} copy-done((f32[1,2,128,128]{3,2,1,0:T(8,128)S(1)}, f32[1,2,128,128]{3,2,1,0:T(8,128)}, u32[]{:S(2)}) %copy-start.3) | copy-done | bytes 131096
  39.5 22.3 %chain.1 = (f32[2,256]{1,0:T(2,128)S(1)}, f32[2,128,128]{2,1,0:T(8,128)}) custom-call(s32[1]{0:T(128)S(6)} %copy.8.count_ref, f32[2,256]{1,0:T(2,128)S(1)} %pad.4.harm_ref, f32[2,128,128]{2,1,0:T(8,128)S(1)} %bitcast.11, f32[2,128,128]{2,1,0:T(8,128)S(1)} %bitcast.12, f32[8,136,256]{2,1,0:T(8,128)S(1)} %bitcast.9), custom_call_target="tpu_custom_call" | custom-call | tf_op jit(solution)/shard_map/chain/pallas_call | solution.py:267
  61.8 9.6 %psum.7 = f32[2,256]{1,0:T(2,128)S(1)} all-reduce(f32[2,256]{1,0:T(2,128)S(1)} %get-tuple-element.4), channel_id=1, replica_groups=mesh['layer'=8,'wave'=4] {'wave'}, use_global_device_ids=true, to_apply=%region_0.1 | all-reduce | flops 512 | bytes 4096 | tf_op jit(solution)/shard_map/psum | solution.py:279
  71.4 0.6 slice_bitcast_fusion
Async XLA Ops:
  7.2 29.3 %all-gather.3.cloned.1.call-start = ((), (), s32[]{:S(2)}) async-start(), calls=%async_computation | async-start | bytes 1253376 | tf_op jit(solution)/shard_map/all_gather | solution.py:266
  8.5 0.9 %copy-start.1 = (f32[1,1,2,128,128]{4,3,2,1,0:T(8,128)S(1)}, f32[1,1,2,128,128]{4,3,2,1,0:T(8,128)}, u32[]{:S(2)}) copy-start(f32[1,1,2,128,128]{4,3,2,1,0:T(8,128)} %param.7) | copy-start | bytes 393220
  9.4 0.7 copy-start.4
  10.1 0.7 copy-start.5
  36.5 1.2 %copy-start = (f32[1088,256]{1,0:T(8,128)S(1)}, f32[1088,256]{1,0:T(8,128)}, u32[]{:S(2)}) copy-start(f32[1088,256]{1,0:T(8,128)} %all-gather.3.cloned.1.call-done) | copy-start | bytes 3342340
  37.7 0.9 %copy-start.2 = (f32[1,1,2,128,128]{4,3,2,1,0:T(8,128)S(1)}, f32[1,1,2,128,128]{4,3,2,1,0:T(8,128)}, u32[]{:S(2)}) copy-start(f32[1,1,2,128,128]{4,3,2,1,0:T(8,128)} %param.7) | copy-start | bytes 393220
  38.6 0.9 %copy-start.3 = (f32[1,2,128,128]{3,2,1,0:T(8,128)S(1)}, f32[1,2,128,128]{3,2,1,0:T(8,128)}, u32[]{:S(2)}) copy-start(f32[1,2,128,128]{3,2,1,0:T(8,128)} %param.11) | copy-start | bytes 393220
Sparse Core Ops, SparseCore 0:
  11.9 24.4 all-gather.2
where the time goes:
time: 79.1 us; the launch traced here: 78.8 us
  waiting for transfers between devices  24.7 us (31%)
  Pallas kernels  23.3 us (29%)
  between operations  14.7 us (19%)
  blocking collectives  9.64 us (12%)
  local copies, waits for them, and re-layouts  6.54 us (8%)
    all_gather x1, waiting for transfers between devices, per_device(): packs = lax.all_gather(pack, 'layer')  24.6 us
    pallas_call x1, Pallas kernels, per_device(): pl.pallas_call(functools.partial(chain_kernel, layers), out_shape=(jax.Sh...  22.3 us
    psum x1, blocking collectives, per_device(): eps_grad = lax.psum(eps_part, 'wave')[:, :2 * n - 1]  9.64 us
    unnamed x12, local copies, waits for them, and re-layouts  5.27 us
  transfers between devices with their start and end apart: 1, of which 1 were waited for; matrix products, arithmetic and copies ran while one was open for 0% of the time, Pallas kernels for 0%

commit v1 on v0

--- a/solution.py
+++ b/solution.py
@@ -12,6 +12,7 @@
 LEVELS = 5
 F32 = jnp.float32
 BF16 = jnp.bfloat16
+MESH = pl.DeviceIdType.MESH
 
 
 def split(x):
@@ -116,37 +117,96 @@
 
 def toeplitz_of(harm_ref, n):
     def one(part):
-        rows = jnp.broadcast_to(harm_ref[part : part + 1, :], (n, 2 * n))
+        harmonics = jnp.concatenate([harm_ref[part : part + 1, :], jnp.zeros((1, 1), F32)], axis=1)
+        rows = jnp.broadcast_to(harmonics, (n, 2 * n))
         rolled = pltpu.roll(rows, n + 1, 1, stride=1, stride_axis=0)
         return rolled[:, :n].T
 
     return jnp.concatenate([one(0), one(1)], axis=1)
 
 
-def sheet_kernel(count_ref, harm_ref, mode_ref, phase_ref, decay_ref, pack_ref):
-    n = mode_ref.shape[-1]
-    count = count_ref[0]
-    toeplitz = toeplitz_of(harm_ref, n)
-    modes = jnp.concatenate([mode_ref[0], mode_ref[1]], axis=1)
-    mask = order_mask(count, n) * (1.0 / (5.0 * math.sqrt(2 * n - 1)))
-    coupled = product(split(toeplitz), split(modes))
-    pack_ref[:n, :] = coupled * jnp.concatenate([mask, mask], axis=1)
-    order = lax.broadcasted_iota(jnp.int32, (1, n), 1) - n // 2
-    window = ((order >= -(count // 2)) & (order < count - count // 2)).astype(F32)
-    magnitude = window * jnp.exp(-decay_ref[...])
-    phase = phase_ref[...]
-    prop = jnp.concatenate([magnitude * jnp.cos(phase), magnitude * jnp.sin(phase)], axis=1)
-    pack_ref[n:, :] = jnp.broadcast_to(prop, (8, 2 * n))
-
-
-def chain_kernel(
-    layers, count_ref, harm_ref, mode_ref, cot_ref, pack_ref, eps_ref, grad_ref,
-    below, back, left, right, bar,
+def kernel(
+    layers, waves, count_ref, harm_in, mode_in, phase_in, decay_in, cot_in, eps_ref, grad_ref,
+    pack_ref, harm_ref, mode_ref, phase_ref, decay_ref, cot_ref, below, back, left, right, bar,
+    eps_slots, in_sem, send_sem, recv_sem, pass_sem, eps_send, eps_recv,
 ):
     n = mode_ref.shape[-1]
     through = TRANSMISSION
     both = through * through
     me = lax.axis_index("layer")
+    wave = lax.axis_index("wave")
+    other_core = me + 1 - 2 * lax.rem(me, 2)
+    far = range(1, layers // 2)
+
+    def ahead(hop):
+        return lax.rem(me + 2 * hop, layers)
+
+    def behind(hop):
+        return lax.rem(me + layers - 2 * hop, layers)
+
+    def wave_ahead(hop):
+        return lax.rem(wave + hop, waves)
+
+    loads = [
+        pltpu.make_async_copy(source, target, in_sem.at[i])
+        for i, (source, target) in enumerate(
+            (
+                (harm_in.at[0], harm_ref),
+                (mode_in.at[0, 0], mode_ref),
+                (phase_in.at[0], phase_ref),
+                (decay_in.at[0], decay_ref),
+                (cot_in.at[0], cot_ref),
+            )
+        )
+    ]
+    for load in loads:
+        load.start()
+    barrier = pltpu.get_barrier_semaphore()
+    peers = [{"layer": other_core}] + [{"layer": ahead(hop)} for hop in far]
+    peers = peers + [{"wave": wave_ahead(hop)} for hop in range(1, waves)]
+    for peer in peers:
+        pl.semaphore_signal(barrier, inc=1, device_id=peer, device_id_type=MESH)
+    for load in loads:
+        load.wait()
+
+    count = count_ref[0]
+    modes = split(jnp.concatenate([mode_ref[0], mode_ref[1]], axis=1))
+    toeplitz = split(toeplitz_of(harm_ref, n))
+    mask = order_mask(count, n) * (1.0 / (5.0 * math.sqrt(2 * n - 1)))
+    mask = jnp.concatenate([mask, mask], axis=1)
+    pack_ref[me, :n, :] = product(toeplitz, modes) * mask
+    order = lax.broadcasted_iota(jnp.int32, (1, n), 1) - n // 2
+    window = ((order >= -(count // 2)) & (order < count - count // 2)).astype(F32)
+    magnitude = window * jnp.exp(-decay_ref[...])
+    phase = phase_ref[...]
+    own = jnp.concatenate([magnitude * jnp.cos(phase), magnitude * jnp.sin(phase)], axis=1)
+    pack_ref[me, n:, :] = jnp.broadcast_to(own, (8, 2 * n))
+
+    def carry(i, sem, to):
+        return pltpu.make_async_remote_copy(
+            src_ref=pack_ref.at[i],
+            dst_ref=pack_ref.at[i],
+            send_sem=sem,
+            recv_sem=recv_sem.at[i],
+            device_id={"layer": to},
+            device_id_type=MESH,
+        )
+
+    pl.semaphore_wait(barrier, len(peers))
+    sends = [carry(me, send_sem.at[hop], ahead(hop)) for hop in far]
+    sends.append(carry(me, send_sem.at[0], other_core))
+    for send in sends:
+        send.start()
+    for hop in far:
+        source = behind(hop)
+        forward = carry(source, pass_sem.at[hop], other_core)
+        forward.wait_recv()
+        forward.start()
+        sends.append(forward)
+    carry(other_core, send_sem.at[0], other_core).wait_recv()
+    for hop in far:
+        source = lax.rem(other_core + layers - 2 * hop, layers)
+        carry(source, pass_sem.at[hop], other_core).wait_recv()
 
     def sheet(i):
         return pack_ref[i, :n, :]
@@ -223,17 +283,12 @@
     sheet_bar = bar[...]
     base_bar, _ = series_back(starts, powers, both * sheet_bar, False)
     sheet_bar = sheet_bar + product(split(start), split(base_bar))
-    mask = order_mask(count_ref[0], n) * (1.0 / (5.0 * math.sqrt(2 * n - 1)))
-    coupled_bar = split(sheet_bar * jnp.concatenate([mask, mask], axis=1))
-    modes = jnp.concatenate([mode_ref[0], mode_ref[1]], axis=1)
-    mode_bar = conj_transpose(product(coupled_bar, split(toeplitz_of(harm_ref, n))))
-    grad_ref[0] = mode_bar[:, :n]
-    grad_ref[1] = mode_bar[:, n:]
+    coupled_bar = split(sheet_bar * mask)
     flip = (
         lax.broadcasted_iota(jnp.int32, (n, n), 0) + lax.broadcasted_iota(jnp.int32, (n, n), 1)
         == n - 1
     ).astype(F32).astype(BF16)
-    flipped = tuple(real_dot(flip, part).astype(BF16) for part in split(modes))
+    flipped = tuple(real_dot(flip, part).astype(BF16) for part in modes)
     toeplitz_bar = product(flipped, coupled_bar)
     zeros = jnp.zeros((n, n), F32)
 
@@ -242,42 +297,87 @@
         rolled = pltpu.roll(wide, 0, 1, stride=1, stride_axis=0)
         return jnp.sum(rolled, axis=0, keepdims=True)
 
-    eps_ref[0:1, :] = fold(toeplitz_bar[:, :n])
-    eps_ref[1:2, :] = -fold(toeplitz_bar[:, n:])
+    eps_slots[wave] = jnp.concatenate(
+        [fold(toeplitz_bar[:, :n]), -fold(toeplitz_bar[:, n:]), jnp.zeros((6, 2 * n), F32)], axis=0
+    )
+
+    def eps_copy(slot, hop, to):
+        return pltpu.make_async_remote_copy(
+            src_ref=eps_slots.at[slot],
+            dst_ref=eps_slots.at[slot],
+            send_sem=eps_send.at[hop],
+            recv_sem=eps_recv.at[slot],
+            device_id={"wave": to},
+            device_id_type=MESH,
+        )
+
+    for hop in range(1, waves):
+        send = eps_copy(wave, hop, wave_ahead(hop))
+        send.start()
+        sends.append(send)
+    mode_bar = conj_transpose(product(coupled_bar, toeplitz))
+    grad_ref[0, 0, 0] = mode_bar[:, :n]
+    grad_ref[0, 0, 1] = mode_bar[:, n:]
+    for hop in range(1, waves):
+        source = lax.rem(wave + waves - hop, waves)
+        eps_copy(source, hop, source).wait_recv()
+    total = eps_slots[0]
+    for slot in range(1, waves):
+        total = total + eps_slots[slot]
+    eps_ref[0] = total[:2, : 2 * n - 1]
+    for send in sends:
+        send.wait_send()
 
 
 def per_device(
-    layers, eps_harmonics, eigen_modes, mode_phase, mode_decay, retained_orders, reflect_cotangent
+    layers,
+    waves,
+    eps_harmonics,
+    eigen_modes,
+    mode_phase,
+    mode_decay,
+    retained_orders,
+    reflect_cotangent,
 ):
     n = eigen_modes.shape[-1]
     vmem = pl.BlockSpec(memory_space=pltpu.VMEM)
     smem = pl.BlockSpec(memory_space=pltpu.SMEM)
-    params = pltpu.CompilerParams(vmem_limit_bytes=48 * 1024 * 1024)
-    harmonics = jnp.pad(eps_harmonics[0], ((0, 0), (0, 1)))
-    modes = eigen_modes[0, 0]
-    pack = pl.pallas_call(
-        sheet_kernel,
-        out_shape=jax.ShapeDtypeStruct((n + 8, 2 * n), F32),
-        in_specs=[smem] + [vmem] * 4,
-        out_specs=vmem,
-        compiler_params=params,
-        name="sheet",
-    )(retained_orders, harmonics, modes, mode_phase[0], mode_decay[0])
-    packs = lax.all_gather(pack, "layer")
-    eps_part, grad = pl.pallas_call(
-        functools.partial(chain_kernel, layers),
+    anywhere = pl.BlockSpec(memory_space=pl.ANY)
+    dma = pltpu.SemaphoreType.DMA
+    wide = pltpu.VMEM((n, 2 * n), F32)
+    return pl.pallas_call(
+        functools.partial(kernel, layers, waves),
         out_shape=(
-            jax.ShapeDtypeStruct((2, 2 * n), F32),
-            jax.ShapeDtypeStruct((2, n, n), F32),
+            jax.ShapeDtypeStruct(eps_harmonics.shape, F32),
+            jax.ShapeDtypeStruct(eigen_modes.shape, F32),
         ),
-        in_specs=[smem] + [vmem] * 4,
+        in_specs=[smem] + [anywhere] * 5,
         out_specs=(vmem, vmem),
-        scratch_shapes=[pltpu.VMEM((n, 2 * n), F32) for _ in range(5)],
-        compiler_params=params,
-        name="chain",
-    )(retained_orders, harmonics, modes, reflect_cotangent[0], packs)
-    eps_grad = lax.psum(eps_part, "wave")[:, : 2 * n - 1]
-    return eps_grad[None], grad[None, None]
+        scratch_shapes=[
+            pltpu.VMEM((layers, n + 8, 2 * n), F32),
+            pltpu.VMEM((2, 2 * n - 1), F32),
+            pltpu.VMEM((2, n, n), F32),
+            pltpu.VMEM((1, n), F32),
+            pltpu.VMEM((1, n), F32),
+            pltpu.VMEM((2, n, n), F32),
+            wide,
+            wide,
+            wide,
+            wide,
+            wide,
+            pltpu.VMEM((waves, 8, 2 * n), F32),
+            dma((5,)),
+            dma((layers,)),
+            dma((layers,)),
+            dma((layers,)),
+            dma((waves,)),
+            dma((waves,)),
+        ],
+        compiler_params=pltpu.CompilerParams(
+            vmem_limit_bytes=48 * 1024 * 1024, collective_id=0, has_side_effects=True
+        ),
+        name="stack",
+    )(retained_orders, eps_harmonics, eigen_modes, mode_phase, mode_decay, reflect_cotangent)
 
 
 def solution(mesh):
@@ -290,7 +390,7 @@
         P("wave", None, None, None),
     )
     return jax.shard_map(
-        functools.partial(per_device, mesh.shape["layer"]),
+        functools.partial(per_device, mesh.shape["layer"], mesh.shape["wave"]),
         mesh=mesh,
         in_specs=placed,
         out_specs=(P("layer", None, None), P("layer", "wave", None, None, None)),

time: 79.1 us -> 42.8 us (0.54)
  waiting for transfers between devices: 24.7 us -> 0 us
  Pallas kernels: 23.3 us -> 37.5 us
  between operations: 14.7 us -> 1.35 us
  blocking collectives: 9.64 us -> 0 us
  local copies, waits for them, and re-layouts: 6.54 us -> 3.73 us
    all_gather x1 -> x0, waiting for transfers between devices: 24.6 us -> none  [per_device(): packs = lax.all_gather(pack, 'layer')]
    pallas_call x2 -> x1, Pallas kernels: 23.3 us -> 37.5 us  [per_device(): pl.pallas_call(functools.partial(kernel, layers, waves), out_shape=(jax.S...]
    psum x1 -> x0, blocking collectives: 9.64 us -> none  [per_device(): eps_grad = lax.psum(eps_part, 'wave')[:, :2 * n - 1]]
    unnamed x12, local copies, waits for them, and re-layouts: 5.27 us -> 3.73 us
  transfers between devices with their start and end apart: 1 -> 0, of which waited for: 1 -> 0; matrix products, arithmetic and copies ran while one was open for 0% -> 0% of each run, Pallas kernels for 0% -> 0%
where the time goes in v1:
time: 42.8 us; the launch traced here: 42.6 us
  Pallas kernels  37.5 us (88%)
  local copies, waits for them, and re-layouts  3.73 us (9%)
  between operations  1.35 us (3%)
    pallas_call x1, Pallas kernels, per_device(): pl.pallas_call(functools.partial(kernel, layers, waves), out_shape=(jax.S...  37.5 us
    unnamed x12, local copies, waits for them, and re-layouts  3.73 us

profile of v1, /device:TPU:7, one launch (start us, length us, event | category | flops | bytes accessed | tf_op | source)
XLA Modules:
  0.0 42.6 jit_solution(3838133387852365009)
XLA Ops:
  0.6 0.0 copy-start.4
  0.6 0.0 copy-start.3
  1.3 0.0 copy-done.4
  1.3 0.0 copy-done.3
  1.3 0.0 copy-start
  1.3 0.9 %copy-done = f32[1,1,2,128,128]{4,3,2,1,0:T(8,128)S(1)} copy-done((f32[1,1,2,128,128]{4,3,2,1,0:T(8,128)S(1)}, f32[1,1,2,128,128]{4,3,2,1,0:T(8,128)}, u32[]{:S(2)}) %copy-start) | copy-done | bytes 131096
  2.2 0.0 copy-start.1
  2.2 0.9 %copy-done.1 = f32[1,2,128,128]{3,2,1,0:T(8,128)S(1)} copy-done((f32[1,2,128,128]{3,2,1,0:T(8,128)S(1)}, f32[1,2,128,128]{3,2,1,0:T(8,128)}, u32[]{:S(2)}) %copy-start.1) | copy-done | bytes 131096
  3.1 0.0 copy-start.2
  3.1 0.7 %copy-done.2 = f32[1,2,255]{2,1,0:T(2,128)S(1)} copy-done((f32[1,2,255]{2,1,0:T(2,128)S(1)}, f32[1,2,255]{2,1,0:T(2,128)}, u32[]{:S(2)}) %copy-start.2) | copy-done | bytes 2064
  3.8 37.5 %stack.1 = (f32[1,2,255]{2,1,0:T(2,128)S(1)}, f32[1,1,2,128,128]{4,3,2,1,0:T(8,128)S(1)}) custom-call(s32[1]{0:T(128)S(6)} %copy.10.count_ref, f32[1,2,255]{2,1,0:T(2,128)S(1)} %copy-done.2, f32[1,1,2,128,128]{4,3,2,1,0:T(8,128)S(1)} %copy-done, f32[1,1,128]{2,1,0:T(1,128)S(1)} %copy-done.3, f32[1,1,128]{2,1,0:T(1,128)S(1)} %copy-done.4, ...), custom_call_target="tpu_custom_call" | custom-call | tf_op jit(solution)/shard_map/stack/pallas_call | solution.py:348
  41.4 0.6 %copy.11 = f32[1,2,255]{2,1,0:T(2,128)} copy(f32[1,2,255]{2,1,0:T(2,128)S(1)} %get-tuple-element.4) | data formatting | bytes 4080
  41.9 0.7 %copy.12 = f32[1,1,2,128,128]{4,3,2,1,0:T(8,128)} copy(f32[1,1,2,128,128]{4,3,2,1,0:T(8,128)S(1)} %get-tuple-element.5) | data formatting | bytes 262144
Async XLA Ops:
  0.6 0.7 %copy-start.4 = (f32[1,1,128]{2,1,0:T(1,128)S(1)}, f32[1,1,128]{2,1,0:T(1,128)}, u32[]{:S(2)}) copy-start(f32[1,1,128]{2,1,0:T(1,128)} %decay_in.1) | copy-start | bytes 1540
  0.6 0.7 %copy-start.3 = (f32[1,1,128]{2,1,0:T(1,128)S(1)}, f32[1,1,128]{2,1,0:T(1,128)}, u32[]{:S(2)}) copy-start(f32[1,1,128]{2,1,0:T(1,128)} %phase_in.1) | copy-start | bytes 1540
  1.3 0.9 %copy-start = (f32[1,1,2,128,128]{4,3,2,1,0:T(8,128)S(1)}, f32[1,1,2,128,128]{4,3,2,1,0:T(8,128)}, u32[]{:S(2)}) copy-start(f32[1,1,2,128,128]{4,3,2,1,0:T(8,128)} %mode_in.1) | copy-start | bytes 393220
  2.2 0.9 %copy-start.1 = (f32[1,2,128,128]{3,2,1,0:T(8,128)S(1)}, f32[1,2,128,128]{3,2,1,0:T(8,128)}, u32[]{:S(2)}) copy-start(f32[1,2,128,128]{3,2,1,0:T(8,128)} %cot_in.1) | copy-start | bytes 393220
  3.1 0.7 %copy-start.2 = (f32[1,2,255]{2,1,0:T(2,128)S(1)}, f32[1,2,255]{2,1,0:T(2,128)}, u32[]{:S(2)}) copy-start(f32[1,2,255]{2,1,0:T(2,128)} %harm_in.1) | copy-start | bytes 6124

commit v2 on v1

--- a/solution.py
+++ b/solution.py
@@ -140,9 +140,6 @@
 
     def ahead(hop):
         return lax.rem(me + 2 * hop, layers)
-
-    def behind(hop):
-        return lax.rem(me + layers - 2 * hop, layers)
 
     def wave_ahead(hop):
         return lax.rem(wave + hop, waves)
@@ -166,7 +163,7 @@
     peers = peers + [{"wave": wave_ahead(hop)} for hop in range(1, waves)]
     for peer in peers:
         pl.semaphore_signal(barrier, inc=1, device_id=peer, device_id_type=MESH)
-    for load in loads:
+    for load in loads[:4]:
         load.wait()
 
     count = count_ref[0]
@@ -193,20 +190,22 @@
         )
 
     pl.semaphore_wait(barrier, len(peers))
-    sends = [carry(me, send_sem.at[hop], ahead(hop)) for hop in far]
-    sends.append(carry(me, send_sem.at[0], other_core))
+    sends = [carry(me, send_sem.at[0], other_core)]
+    sends = sends + [carry(me, send_sem.at[hop], ahead(hop)) for hop in far]
     for send in sends:
         send.start()
-    for hop in far:
-        source = behind(hop)
-        forward = carry(source, pass_sem.at[hop], other_core)
+    carry(other_core, send_sem.at[0], other_core).wait_recv()
+    core = lax.rem(me, 2)
+    pair = me // 2
+    pairs = layers // 2
+
+    def receive(q):
+        near = 2 * q + core
+        forward = carry(near, pass_sem.at[q], other_core)
         forward.wait_recv()
         forward.start()
-        sends.append(forward)
-    carry(other_core, send_sem.at[0], other_core).wait_recv()
-    for hop in far:
-        source = lax.rem(other_core + layers - 2 * hop, layers)
-        carry(source, pass_sem.at[hop], other_core).wait_recv()
+        across = 2 * q + 1 - core
+        carry(across, pass_sem.at[q], other_core).wait_recv()
 
     def sheet(i):
         return pack_ref[i, :n, :]
@@ -214,32 +213,47 @@
     def prop(i):
         return pack_ref[i, n : n + 1, :]
 
-    below[...] = scaled(outer(prop(layers - 2)), sheet(layers - 1))
-
-    def go_up(step, carry):
-        i = layers - 2 - step
+    def go_up(i, token):
         here = sheet(i)
-        start = below[...]
+        start = scaled(outer(prop(i)), below[...])
         base = product(split(here), split(start))
         value, _, _ = series(start, base)
-        below[...] = scaled(outer(prop(i - 1)), here + both * value)
-        return carry
-
-    lax.fori_loop(0, jnp.maximum(layers - 2 - me, 0), go_up, 0)
-
-    @pl.when(me == layers - 1)
-    def _():
-        below[...] = jnp.zeros_like(below)
-
-    unit = (
-        lax.broadcasted_iota(jnp.int32, (n, n), 0) == lax.broadcasted_iota(jnp.int32, (n, n), 1)
-    ).astype(F32)
-    unit = jnp.concatenate([unit, unit], axis=1)
-    back[...] = scaled(outer(prop(0)), sheet(0))
-    left[...] = through * unit * prop(0)
-    right[...] = through * unit * prop(0)
-
-    def go_down(i, carry):
+        below[...] = here + both * value
+        return token
+
+    def pair_up(step, token):
+        q = pairs - 1 - step
+        receive(q)
+
+        @pl.when(step == 0)
+        def _():
+            below[...] = sheet(layers - 1)
+
+        first = jnp.where(step == 0, 1, 0)
+        lax.fori_loop(first, 2, lambda k, t: go_up(2 * q + 1 - k, t), 0)
+        return token
+
+    lax.fori_loop(0, pairs - 1 - pair, pair_up, 0)
+
+    @pl.when(pair == pairs - 1)
+    def _():
+        below[...] = sheet(layers - 1)
+
+    @pl.when((core == 0) & (pair < pairs - 1))
+    def _():
+        go_up(me + 1, 0)
+
+    def first_layer():
+        unit = (
+            lax.broadcasted_iota(jnp.int32, (n, n), 0)
+            == lax.broadcasted_iota(jnp.int32, (n, n), 1)
+        ).astype(F32)
+        unit = jnp.concatenate([unit, unit], axis=1)
+        back[...] = scaled(outer(prop(0)), sheet(0))
+        left[...] = through * unit * prop(0)
+        right[...] = through * unit * prop(0)
+
+    def go_down(i, token):
         here = split(sheet(i))
         value, into, out = back[...], left[...], right[...]
         value_parts = split(value)
@@ -260,29 +274,62 @@
         back[...] = scaled(outer(p), sheet(i) + both * value)
         left[...] = through * scaled(into, spread_rows(p))
         right[...] = through * scaled(spread_columns(p), out)
-        return carry
-
-    lax.fori_loop(1, jnp.maximum(me, 1), go_down, 0)
-
-    here = sheet(me)
-    start = below[...]
-    base = product(split(here), split(start))
-    value, starts, powers = series(start, base)
-    reflection = here + both * value
-    bar[...] = conj_transpose(jnp.concatenate([cot_ref[0], cot_ref[1]], axis=1))
-
-    @pl.when(me > 0)
-    def _():
-        above = split(back[...])
-        above_base = product(above, split(reflection))
-        _, above_starts, above_powers = series(reflection, above_base)
-        inner = product(split(product(split(right[...]), split(bar[...]))), split(left[...]))
-        base_bar, start_bar = series_back(above_starts, above_powers, inner, True)
-        bar[...] = start_bar + product(split(base_bar), above)
+        return token
+
+    def pair_down(q, token):
+        receive(q)
+
+        @pl.when(q == 0)
+        def _():
+            first_layer()
+
+        first = jnp.where(q == 0, 1, 0)
+        lax.fori_loop(2 * q + first, 2 * q + 2, go_down, 0)
+        return token
+
+    lax.fori_loop(0, pair, pair_down, 0)
+
+    @pl.when(me == 1)
+    def _():
+        first_layer()
+
+    @pl.when((core == 1) & (pair > 0))
+    def _():
+        go_down(me - 1, 0)
+
+    loads[4].wait()
+
+    def own_layer(has_below):
+        reflection = here = sheet(me)
+        if has_below:
+            start = scaled(outer(prop(me)), below[...])
+            base = product(split(here), split(start))
+            value, starts, powers = series(start, base)
+            reflection = here + both * value
+        bar[...] = conj_transpose(jnp.concatenate([cot_ref[0], cot_ref[1]], axis=1))
+
+        @pl.when(me > 0)
+        def _():
+            above = split(back[...])
+            above_base = product(above, split(reflection))
+            _, above_starts, above_powers = series(reflection, above_base)
+            inner = product(split(product(split(right[...]), split(bar[...]))), split(left[...]))
+            base_bar, start_bar = series_back(above_starts, above_powers, inner, True)
+            bar[...] = start_bar + product(split(base_bar), above)
+
+        if has_below:
+            base_bar, _ = series_back(starts, powers, both * bar[...], False)
+            bar[...] += product(split(start), split(base_bar))
+
+    @pl.when(me < layers - 1)
+    def _():
+        own_layer(True)
+
+    @pl.when(me == layers - 1)
+    def _():
+        own_layer(False)
 
     sheet_bar = bar[...]
-    base_bar, _ = series_back(starts, powers, both * sheet_bar, False)
-    sheet_bar = sheet_bar + product(split(start), split(base_bar))
     coupled_bar = split(sheet_bar * mask)
     flip = (
         lax.broadcasted_iota(jnp.int32, (n, n), 0) + lax.broadcasted_iota(jnp.int32, (n, n), 1)
@@ -327,6 +374,9 @@
     eps_ref[0] = total[:2, : 2 * n - 1]
     for send in sends:
         send.wait_send()
+    for hop in far:
+        q = lax.rem(pair + hop, pairs)
+        carry(2 * q + core, pass_sem.at[q], other_core).wait_send()
 
 
 def per_device(
@@ -342,7 +392,7 @@
     n = eigen_modes.shape[-1]
     vmem = pl.BlockSpec(memory_space=pltpu.VMEM)
     smem = pl.BlockSpec(memory_space=pltpu.SMEM)
-    anywhere = pl.BlockSpec(memory_space=pl.ANY)
+    hbm = pl.BlockSpec(memory_space=pltpu.HBM)
     dma = pltpu.SemaphoreType.DMA
     wide = pltpu.VMEM((n, 2 * n), F32)
     return pl.pallas_call(
@@ -351,7 +401,7 @@
             jax.ShapeDtypeStruct(eps_harmonics.shape, F32),
             jax.ShapeDtypeStruct(eigen_modes.shape, F32),
         ),
-        in_specs=[smem] + [anywhere] * 5,
+        in_specs=[smem] + [hbm] * 5,
         out_specs=(vmem, vmem),
         scratch_shapes=[
             pltpu.VMEM((layers, n + 8, 2 * n), F32),

time: 42.8 us -> 42.1 us (0.984); the launches traced: 42.6 us -> 41.3 us
  Pallas kernels: 37.5 us -> 36.2 us
    pallas_call x1, Pallas kernels: 37.5 us -> 36.2 us  [per_device(): pl.pallas_call(functools.partial(kernel, layers, waves), out_shape=(jax.S...]
where the time goes in v2:
time: 42.1 us; the launch traced here: 41.3 us
  Pallas kernels  36.2 us (86%)
  local copies, waits for them, and re-layouts  3.73 us (9%)
  between operations  1.35 us (3%)
    pallas_call x1, Pallas kernels, per_device(): pl.pallas_call(functools.partial(kernel, layers, waves), out_shape=(jax.S...  36.2 us
    unnamed x12, local copies, waits for them, and re-layouts  3.73 us

profile of v2, /device:TPU:7, one launch (start us, length us, event | category | flops | bytes accessed | tf_op | source)
XLA Modules:
  0.0 41.3 jit_solution(3254430383576235566)
XLA Ops:
  0.6 0.0 copy-start.4
  0.6 0.0 copy-start.3
  1.3 0.0 copy-done.4
  1.3 0.0 copy-done.3
  1.3 0.0 copy-start
  1.3 0.9 %copy-done = f32[1,1,2,128,128]{4,3,2,1,0:T(8,128)S(1)} copy-done((f32[1,1,2,128,128]{4,3,2,1,0:T(8,128)S(1)}, f32[1,1,2,128,128]{4,3,2,1,0:T(8,128)}, u32[]{:S(2)}) %copy-start) | copy-done | bytes 131096
  2.2 0.0 copy-start.1
  2.2 0.9 %copy-done.1 = f32[1,2,128,128]{3,2,1,0:T(8,128)S(1)} copy-done((f32[1,2,128,128]{3,2,1,0:T(8,128)S(1)}, f32[1,2,128,128]{3,2,1,0:T(8,128)}, u32[]{:S(2)}) %copy-start.1) | copy-done | bytes 131096
  3.1 0.0 copy-start.2
  3.1 0.7 %copy-done.2 = f32[1,2,255]{2,1,0:T(2,128)S(1)} copy-done((f32[1,2,255]{2,1,0:T(2,128)S(1)}, f32[1,2,255]{2,1,0:T(2,128)}, u32[]{:S(2)}) %copy-start.2) | copy-done | bytes 2064
  3.8 36.2 %stack.1 = (f32[1,2,255]{2,1,0:T(2,128)S(1)}, f32[1,1,2,128,128]{4,3,2,1,0:T(8,128)S(1)}) custom-call(s32[1]{0:T(128)S(6)} %copy.10.count_ref, f32[1,2,255]{2,1,0:T(2,128)S(1)} %copy-done.2, f32[1,1,2,128,128]{4,3,2,1,0:T(8,128)S(1)} %copy-done, f32[1,1,128]{2,1,0:T(1,128)S(1)} %copy-done.3, f32[1,1,128]{2,1,0:T(1,128)S(1)} %copy-done.4, ...), custom_call_target="tpu_custom_call" | custom-call | tf_op jit(solution)/shard_map/stack/pallas_call | solution.py:398
  40.1 0.6 %copy.11 = f32[1,2,255]{2,1,0:T(2,128)} copy(f32[1,2,255]{2,1,0:T(2,128)S(1)} %get-tuple-element.4) | data formatting | bytes 4080
  40.6 0.7 %copy.12 = f32[1,1,2,128,128]{4,3,2,1,0:T(8,128)} copy(f32[1,1,2,128,128]{4,3,2,1,0:T(8,128)S(1)} %get-tuple-element.5) | data formatting | bytes 262144
Async XLA Ops:
  0.6 0.7 %copy-start.4 = (f32[1,1,128]{2,1,0:T(1,128)S(1)}, f32[1,1,128]{2,1,0:T(1,128)}, u32[]{:S(2)}) copy-start(f32[1,1,128]{2,1,0:T(1,128)} %decay_in.1) | copy-start | bytes 1540
  0.6 0.7 %copy-start.3 = (f32[1,1,128]{2,1,0:T(1,128)S(1)}, f32[1,1,128]{2,1,0:T(1,128)}, u32[]{:S(2)}) copy-start(f32[1,1,128]{2,1,0:T(1,128)} %phase_in.1) | copy-start | bytes 1540
  1.3 0.9 %copy-start = (f32[1,1,2,128,128]{4,3,2,1,0:T(8,128)S(1)}, f32[1,1,2,128,128]{4,3,2,1,0:T(8,128)}, u32[]{:S(2)}) copy-start(f32[1,1,2,128,128]{4,3,2,1,0:T(8,128)} %mode_in.1) | copy-start | bytes 393220
  2.2 0.9 %copy-start.1 = (f32[1,2,128,128]{3,2,1,0:T(8,128)S(1)}, f32[1,2,128,128]{3,2,1,0:T(8,128)}, u32[]{:S(2)}) copy-start(f32[1,2,128,128]{3,2,1,0:T(8,128)} %cot_in.1) | copy-start | bytes 393220
  3.1 0.7 %copy-start.2 = (f32[1,2,255]{2,1,0:T(2,128)S(1)}, f32[1,2,255]{2,1,0:T(2,128)}, u32[]{:S(2)}) copy-start(f32[1,2,255]{2,1,0:T(2,128)} %harm_in.1) | copy-start | bytes 6124

commit v3 on v2

--- a/solution.py
+++ b/solution.py
@@ -46,8 +46,16 @@
     ]
 
 
+def products_of_one(left, weight):
+    return products([left], weight)[0]
+
+
 def product(left, right):
-    return products([left], weights(right))[0]
+    return products_of_one(left, weights(right))
+
+
+def single(left, weight):
+    return real_dot(left[0], weight[0])
 
 
 def scaled(a, b):
@@ -84,10 +92,13 @@
         starts.append(value_parts)
         powers.append(power_parts)
         weight = weights(power_parts)
-        if level + 1 < LEVELS:
+        if level + 2 < LEVELS:
             step, power = products([value_parts, power_parts], weight)
+        elif level + 1 < LEVELS:
+            (step,) = products([value_parts], weight)
+            power = single(power_parts, weight)
         else:
-            (step,) = products([value_parts], weight)
+            step = single(value_parts, weight)
         value = value + step
     return value, starts, powers
 
@@ -102,7 +113,8 @@
             total = total + product(bar_parts, powers[level])
             total = total + product(powers[level], bar_parts)
         if level > 0 or need_start:
-            cotangent = cotangent + product(powers[level], parts)
+            form = single if level + 1 == LEVELS else products_of_one
+            cotangent = cotangent + form(powers[level], weights(parts))
         power_bar = total
     return power_bar, cotangent
 
@@ -262,14 +274,23 @@
         for level in range(LEVELS):
             power_parts, other_parts = split(power), split(other)
             weight = weights(power_parts)
-            last = level + 1 == LEVELS
-            lefts = [split(value), split(into)] + ([] if last else [power_parts])
-            steps = products(lefts, weight)
-            value, into = value + steps[0], into + steps[1]
-            out = out + product(other_parts, split(out))
-            if not last:
+            out_weight = weights(split(out))
+            if level + 1 == LEVELS:
+                value = value + single(split(value), weight)
+                into = into + single(split(into), weight)
+                out = out + single(other_parts, out_weight)
+                break
+            out = out + products_of_one(other_parts, out_weight)
+            lefts = [split(value), split(into)]
+            if level + 2 == LEVELS:
+                steps = products(lefts, weight)
+                power = single(power_parts, weight)
+                other = single(other_parts, weights(other_parts))
+            else:
+                steps = products(lefts + [power_parts], weight)
                 power = steps[2]
                 other = product(other_parts, other_parts)
+            value, into = value + steps[0], into + steps[1]
         p = prop(i)
         back[...] = scaled(outer(p), sheet(i) + both * value)
         left[...] = through * scaled(into, spread_rows(p))

time: 42.1 us -> 40.7 us (0.967)
  the two profiles are of different devices: /device:TPU:7 before, /device:TPU:6 now
where the time goes in v3:
time: 40.7 us; the launch traced here: 40.5 us
  Pallas kernels  35.5 us (87%)
  local copies, waits for them, and re-layouts  3.73 us (9%)
  between operations  1.35 us (3%)
    pallas_call x1, Pallas kernels, per_device(): pl.pallas_call(functools.partial(kernel, layers, waves), out_shape=(jax.S...  35.5 us
    unnamed x12, local copies, waits for them, and re-layouts  3.73 us

profile of v3, /device:TPU:6, one launch (start us, length us, event | category | flops | bytes accessed | tf_op | source)
XLA Modules:
  0.0 40.5 jit_solution(12606035819742109607)
XLA Ops:
  0.6 0.0 copy-start.4
  0.6 0.0 copy-start.3
  1.3 0.0 copy-done.4
  1.3 0.0 copy-done.3
  1.3 0.0 copy-start
  1.3 0.9 %copy-done = f32[1,1,2,128,128]{4,3,2,1,0:T(8,128)S(1)} copy-done((f32[1,1,2,128,128]{4,3,2,1,0:T(8,128)S(1)}, f32[1,1,2,128,128]{4,3,2,1,0:T(8,128)}, u32[]{:S(2)}) %copy-start) | copy-done | bytes 131096
  2.2 0.0 copy-start.1
  2.2 0.9 %copy-done.1 = f32[1,2,128,128]{3,2,1,0:T(8,128)S(1)} copy-done((f32[1,2,128,128]{3,2,1,0:T(8,128)S(1)}, f32[1,2,128,128]{3,2,1,0:T(8,128)}, u32[]{:S(2)}) %copy-start.1) | copy-done | bytes 131096
  3.1 0.0 copy-start.2
  3.1 0.7 %copy-done.2 = f32[1,2,255]{2,1,0:T(2,128)S(1)} copy-done((f32[1,2,255]{2,1,0:T(2,128)S(1)}, f32[1,2,255]{2,1,0:T(2,128)}, u32[]{:S(2)}) %copy-start.2) | copy-done | bytes 2064
  3.8 35.5 %stack.1 = (f32[1,2,255]{2,1,0:T(2,128)S(1)}, f32[1,1,2,128,128]{4,3,2,1,0:T(8,128)S(1)}) custom-call(s32[1]{0:T(128)S(6)} %copy.10.count_ref, f32[1,2,255]{2,1,0:T(2,128)S(1)} %copy-done.2, f32[1,1,2,128,128]{4,3,2,1,0:T(8,128)S(1)} %copy-done, f32[1,1,128]{2,1,0:T(1,128)S(1)} %copy-done.3, f32[1,1,128]{2,1,0:T(1,128)S(1)} %copy-done.4, ...), custom_call_target="tpu_custom_call" | custom-call | tf_op jit(solution)/shard_map/stack/pallas_call | solution.py:419
  39.3 0.6 %copy.11 = f32[1,2,255]{2,1,0:T(2,128)} copy(f32[1,2,255]{2,1,0:T(2,128)S(1)} %get-tuple-element.4) | data formatting | bytes 4080
  39.9 0.7 %copy.12 = f32[1,1,2,128,128]{4,3,2,1,0:T(8,128)} copy(f32[1,1,2,128,128]{4,3,2,1,0:T(8,128)S(1)} %get-tuple-element.5) | data formatting | bytes 262144
Async XLA Ops:
  0.6 0.7 %copy-start.4 = (f32[1,1,128]{2,1,0:T(1,128)S(1)}, f32[1,1,128]{2,1,0:T(1,128)}, u32[]{:S(2)}) copy-start(f32[1,1,128]{2,1,0:T(1,128)} %decay_in.1) | copy-start | bytes 1540
  0.6 0.7 %copy-start.3 = (f32[1,1,128]{2,1,0:T(1,128)S(1)}, f32[1,1,128]{2,1,0:T(1,128)}, u32[]{:S(2)}) copy-start(f32[1,1,128]{2,1,0:T(1,128)} %phase_in.1) | copy-start | bytes 1540
  1.3 0.9 %copy-start = (f32[1,1,2,128,128]{4,3,2,1,0:T(8,128)S(1)}, f32[1,1,2,128,128]{4,3,2,1,0:T(8,128)}, u32[]{:S(2)}) copy-start(f32[1,1,2,128,128]{4,3,2,1,0:T(8,128)} %mode_in.1) | copy-start | bytes 393220
  2.2 0.9 %copy-start.1 = (f32[1,2,128,128]{3,2,1,0:T(8,128)S(1)}, f32[1,2,128,128]{3,2,1,0:T(8,128)}, u32[]{:S(2)}) copy-start(f32[1,2,128,128]{3,2,1,0:T(8,128)} %cot_in.1) | copy-start | bytes 393220
  3.1 0.7 %copy-start.2 = (f32[1,2,255]{2,1,0:T(2,128)S(1)}, f32[1,2,255]{2,1,0:T(2,128)}, u32[]{:S(2)}) copy-start(f32[1,2,255]{2,1,0:T(2,128)} %harm_in.1) | copy-start | bytes 6124
